TPU v7x, 128 devices: a whole 4x4x4 slice. The times are simulated.
128 devices in a mesh: lon: 16 (over x_hi, z, core), lat: 8 (over x_lo, y).
Axes of the slice: x: 4 (x_hi: 2, x_lo: 2; x = x_hi * 2 + x_lo), y: 4, z: 4, core: 2. Of those that a mesh axis runs over, the one named last changes fastest.
Arguments:
- state: bfloat16 [16, 8, 64, 512, 128], P('lon', 'lat'), may hold values from -6 to 6
- conv_w: bfloat16 [3, 8, 16, 16], replicated, may hold values from -0.875 to 0.875
- readout: float32 [128, 8], replicated, may hold values from -0.5 to 0.5
- kernel: float32 [256, 64, 8], replicated, may hold values from -0.25 to 0.25
- cross_col: int32 [16, 8, 8, 256], P('lon', 'lat'), may hold values from 0 to 511
- seg_count: int32 [16, 8, 256], P('lon', 'lat'), may hold values from 1 to 8
- seg_len: float32 [16, 8, 8, 256], P('lon', 'lat'), may hold values from 0.25 to 1
- observed: float32 [16, 8, 256, 256], P('lon', 'lat'), may hold values from -8 to 8
- obs_err: float32 [16, 8, 256, 256], P('lon', 'lat'), may hold values from 0.5 to 2
Outputs:
- grad_state: bfloat16 [16, 8, 64, 512, 128], P('lon', 'lat')
- bending: float32 [16, 8, 256, 256], P('lon', 'lat')
- grad_conv: float32 [3, 8, 16, 16], replicated
Inputs may be any that keep to these rules, and one draw needn't show every extreme that they name: `cross_col`: a column of the crossed tile.
All inputs are finite; a program needn't handle non-finite values.
Results may differ from a plain program's by a relative error of at most 0.0037.
The roundings to bfloat16 on the way count: a program that leaves them out, or rounds other values in their place, can miss the bound.
Values sent between devices are 32-bit elements; how exact they have to be, the bound alone decides.
A program may use at most 192 MiB of HBM per device.

v0:
```python
import jax
import jax.numpy as jnp
from jax import lax
from jax.sharding import PartitionSpec as P


def from_behind(value, axis, steps):
    count = lax.axis_size(axis)
    pairs = [(source, (source + steps) % count) for source in range(count)]
    return lax.ppermute(value, axis, pairs)


def block_weights(conv_w):
    taps, groups, width, _ = conv_w.shape
    eye = jnp.eye(groups, dtype=jnp.float32)
    full = conv_w.astype(jnp.float32)[:, :, :, None, :] * eye[None, :, None, :, None]
    return full.reshape(taps, groups * width, groups * width).astype(jnp.bfloat16)


def on_device(state, conv_w, readout, kernel, cross_col, seg_count, seg_len, observed, obs_err):
    column = state[0, 0]
    levels = column.shape[0]
    ncols = column.shape[1]
    taps = conv_w.shape[0]
    groups = conv_w.shape[1]
    width = conv_w.shape[2]
    wide = block_weights(conv_w)
    padded = jnp.pad(column, ((1, 1), (0, 0), (0, 0)))
    act = jnp.zeros(column.shape, jnp.float32)
    for tap in range(taps):
        act = act + jnp.einsum(
            "lci,ij->lcj", padded[tap : tap + levels], wide[tap], preferred_element_type=jnp.float32
        )
    feat = jax.nn.silu(act)
    profile = jnp.einsum("lcj,jn->cln", feat, readout, precision=lax.Precision.HIGHEST).reshape(
        ncols, -1
    )
    span = cross_col.shape[2]
    rays = cross_col.shape[3]
    lon_n = lax.axis_size("lon")
    here = lax.axis_index("lon")
    every = lax.all_gather(seg_count, "lon", axis=0, tiled=True)[:, 0, :]
    offsets = jnp.arange(span, dtype=jnp.int32)
    owners = (here - offsets) % lon_n
    counts = jnp.take(every, owners, axis=0)
    weight = seg_len[0, 0] * (offsets[:, None] < counts).astype(jnp.float32)
    places = cross_col[0, 0].reshape(-1)
    sampled = jnp.take(profile, places, axis=0).reshape(span, rays, -1) * weight[:, :, None]
    kflat = kernel.reshape(kernel.shape[0], -1)
    carried = sampled[span - 1]
    for step in range(span - 2, -1, -1):
        carried = from_behind(carried, "lon", -1) + sampled[step]
    bending = jnp.einsum("rq,kq->rk", carried, kflat, precision=lax.Precision.HIGHEST)
    adjoint = (bending - observed[0, 0]) / (obs_err[0, 0] * obs_err[0, 0])
    current = jnp.dot(adjoint, kflat, precision=lax.Precision.HIGHEST)
    held = [current]
    for step in range(1, span):
        current = from_behind(current, "lon", 1)
        held.append(current)
    back = jnp.stack(held)
    back = back * weight[:, :, None]
    dprofile = (
        jnp.zeros((ncols, back.shape[2]), jnp.float32)
        .at[places]
        .add(back.reshape(-1, back.shape[2]))
    )
    dfeat = jnp.einsum(
        "cln,jn->lcj", dprofile.reshape(ncols, levels, -1), readout, precision=lax.Precision.HIGHEST
    )
    sig = jax.nn.sigmoid(act)
    dact = (dfeat * sig * (1.0 + act * (1.0 - sig))).astype(jnp.bfloat16)
    dpad = jnp.pad(dact, ((1, 1), (0, 0), (0, 0)))
    grad_x = jnp.zeros(column.shape, jnp.float32)
    grads = []
    for tap in range(taps):
        grad_x = grad_x + jnp.einsum(
            "lcj,ij->lci",
            dpad[2 - tap : 2 - tap + levels],
            wide[tap],
            preferred_element_type=jnp.float32,
        )
        grads.append(
            jnp.einsum(
                "lci,lcj->ij", padded[tap : tap + levels], dact, preferred_element_type=jnp.float32
            )
        )
    grad_w = jnp.stack(grads).reshape(taps, groups, width, groups, width)
    eye = jnp.eye(groups, dtype=jnp.float32)
    grouped = jnp.einsum("tgahb,gh->tgab", grad_w, eye)
    grad_conv = lax.psum(grouped, ("lon", "lat"))
    return (grad_x.astype(jnp.bfloat16)[None, None], bending[None, None], grad_conv)


def solution(mesh):
    in_specs = (
        P("lon", "lat", None, None, None),
        P(),
        P(),
        P(),
        P("lon", "lat", None, None),
        P("lon", "lat", None),
        P("lon", "lat", None, None),
        P("lon", "lat", None, None),
        P("lon", "lat", None, None),
    )
    out_specs = (P("lon", "lat", None, None, None), P("lon", "lat", None, None), P())
    return jax.shard_map(
        on_device, mesh=mesh, in_specs=in_specs, out_specs=out_specs, check_vma=False
    )
```

profile of v0, /device:TPU:1, one launch (start us, length us, event | category | flops | bytes accessed | tf_op | source)
XLA Modules:
  0.0 433.3 jit_solution(11439077147525505158)
XLA Ops:
  2.5 11.4 %fusion.8 = f32[64,512,128]{2,1,0:T(8,128)} fusion(bf16[1,1,64,512,128]{4,3,2,1,0:T(8,128)(2,1)} %param.9, bf16[3,128,128]{2,1,0:T(8,128)(2,1)S(1)} %multiply_convert_fusion), kind=kOutput, calls=%fused_computation.15 | convolution fusion | flops 1056964608 | bytes 25198592 | tf_op jit(solution)/shard_map/lci,ij->lcj/dot_general | solution.py:31
  14.0 11.4 %fusion.12 = f32[128,64,512]{0,2,1:T(8,128)} fusion(bf16[1,1,64,512,128]{4,3,2,1,0:T(8,128)(2,1)} %param.9, bf16[3,128,128]{2,1,0:T(8,128)(2,1)S(1)} %multiply_convert_fusion), kind=kOutput, calls=%fused_computation.19 | convolution fusion | flops 1073741824 | bytes 25198592 | tf_op jit(solution)/shard_map/lci,ij->lcj/dot_general | solution.py:31
  25.5 21.0 %fusion.2 = f32[64,512,128]{2,1,0:T(8,128)} fusion(f32[64,512,128]{2,1,0:T(8,128)} %fusion.8, f32[128,64,512]{0,2,1:T(8,128)} %fusion.12, bf16[1,1,64,512,128]{4,3,2,1,0:T(8,128)(2,1)} %param.9, bf16[3,128,128]{2,1,0:T(8,128)(2,1)S(1)} %multiply_convert_fusion), kind=kOutput, calls=%fused_computation.7 | convolution fusion | flops 1065353216 | bytes 58753024 | tf_op jit(solution)/shard_map/lci,ij->lcj/dot_general | solution.py:31
  46.5 21.1 %fusion.20 = f32[512,512]{0,1:T(8,128)S(1)} fusion(f32[64,512,128]{2,1,0:T(8,128)} %fusion.2, f32[128,8]{0,1:T(8,128)S(1)} %copy-done.9), kind=kOutput, calls=%fused_computation.30 | convolution fusion | flops 419430400 | bytes 17829888 | tf_op jit(solution)/shard_map/lcj,jn->cln/dot_general | solution.py:35
  68.0 26.7 %all_gather.3 = s32[16,1,256]{2,1,0:T(1,128)S(1)} all-gather(s32[1,1,256]{2,1,0:T(1,128)S(1)} %copy-done.8), channel_id=1, replica_groups=mesh['lon'=16,'lat'=8] {'lon'}, dimensions={0}, use_global_device_ids=true | all-gather | bytes 17408 | tf_op jit(solution)/shard_map/all_gather | solution.py:42
  94.7 8.9 %gather_fusion = f32[2048,512]{1,0:T(8,128)} fusion(f32[512,512]{1,0:T(8,128)S(1)} %copy.40, s32[2048]{0:T(1024)S(1)} %broadcast_clamp_fusion), kind=kCustom, calls=%fused_computation | custom fusion | bytes 8396800 | tf_op jit(solution)/shard_map/jit(_take)/gather | solution.py:48
  104.3 2.7 select_multiply_fusion
  107.2 8.4 %collective-permute-done = f32[256,512]{1,0:T(8,128)S(1)} collective-permute-done((f32[256,512]{1,0:T(8,128)S(1)}, f32[256,512]{1,0:T(8,128)S(1)}, u32[]{:S(2)}, u32[]{:S(2)}) %collective-permute-start) | collective-permute-done | bytes 524320 | tf_op jit(solution)/shard_map/ppermute | solution.py:10
  115.8 8.6 %collective-permute-done.1 = f32[256,512]{1,0:T(8,128)S(1)} collective-permute-done((f32[256,512]{1,0:T(8,128)S(1)}, f32[256,512]{1,0:T(8,128)S(1)}, u32[]{:S(2)}, u32[]{:S(2)}) %collective-permute-start.1) | collective-permute-done | bytes 524320 | tf_op jit(solution)/shard_map/ppermute | solution.py:10
  126.5 6.7 %collective-permute-done.2 = f32[256,512]{1,0:T(8,128)S(1)} collective-permute-done((f32[256,512]{1,0:T(8,128)S(1)}, f32[256,512]{1,0:T(8,128)S(1)}, u32[]{:S(2)}, u32[]{:S(2)}) %collective-permute-start.2) | collective-permute-done | bytes 524320 | tf_op jit(solution)/shard_map/ppermute | solution.py:10
  133.3 5.6 %collective-permute-start.3 = (f32[256,512]{1,0:T(8,128)S(1)}, f32[256,512]{1,0:T(8,128)S(1)}, u32[]{:S(2)}, u32[]{:S(2)}) collective-permute-start(f32[256,512]{1,0:T(8,128)S(1)} %fusion.39), channel_id=1, source_target_pairs={{0,120},{8,0},{16,8},{24,16},{32,24},{40,32},{48,40},{56,48},{64,5... | collective-permute-start | bytes 1572872 | tf_op jit(solution)/shard_map/ppermute | solution.py:10
  138.9 3.1 collective-permute-done.3
  142.0 9.2 %collective-permute-start.4 = (f32[256,512]{1,0:T(8,128)S(1)}, f32[256,512]{1,0:T(8,128)S(1)}, u32[]{:S(2)}, u32[]{:S(2)}) collective-permute-start(f32[256,512]{1,0:T(8,128)S(1)} %fusion.38), channel_id=1, source_target_pairs={{0,120},{8,0},{16,8},{24,16},{32,24},{40,32},{48,40},{56,48},{64,5... | collective-permute-start | bytes 1572872 | tf_op jit(solution)/shard_map/ppermute | solution.py:10
  152.9 10.8 %collective-permute-start.5 = (f32[256,512]{1,0:T(8,128)S(1)}, f32[256,512]{1,0:T(8,128)S(1)}, u32[]{:S(2)}, u32[]{:S(2)}) collective-permute-start(f32[256,512]{1,0:T(8,128)S(1)} %fusion.37), channel_id=1, source_target_pairs={{0,120},{8,0},{16,8},{24,16},{32,24},{40,32},{48,40},{56,48},{64,5... | collective-permute-start | bytes 1572872 | tf_op jit(solution)/shard_map/ppermute | solution.py:10
  165.2 11.0 %collective-permute-start.6 = (f32[256,512]{1,0:T(8,128)S(1)}, f32[256,512]{1,0:T(8,128)S(1)}, u32[]{:S(2)}, u32[]{:S(2)}) collective-permute-start(f32[256,512]{1,0:T(8,128)S(1)} %fusion.36), channel_id=1, source_target_pairs={{0,120},{8,0},{16,8},{24,16},{32,24},{40,32},{48,40},{56,48},{64,5... | collective-permute-start | bytes 1572872 | tf_op jit(solution)/shard_map/ppermute | solution.py:10
  179.9 12.1 %collective-permute-done.7 = f32[256,512]{1,0:T(8,128)S(1)} collective-permute-done((f32[256,512]{1,0:T(8,128)S(1)}, f32[256,512]{1,0:T(8,128)S(1)}, u32[]{:S(2)}, u32[]{:S(2)}) %collective-permute-start.7) | collective-permute-done | bytes 524320 | tf_op jit(solution)/shard_map/ppermute | solution.py:10
  191.9 12.4 %collective-permute-done.8 = f32[256,512]{1,0:T(8,128)S(1)} collective-permute-done((f32[256,512]{1,0:T(8,128)S(1)}, f32[256,512]{1,0:T(8,128)S(1)}, u32[]{:S(2)}, u32[]{:S(2)}) %collective-permute-start.8) | collective-permute-done | bytes 524320 | tf_op jit(solution)/shard_map/ppermute | solution.py:10
  204.3 12.2 %collective-permute-done.9 = f32[256,512]{1,0:T(8,128)S(1)} collective-permute-done((f32[256,512]{1,0:T(8,128)S(1)}, f32[256,512]{1,0:T(8,128)S(1)}, u32[]{:S(2)}, u32[]{:S(2)}) %collective-permute-start.9) | collective-permute-done | bytes 524320 | tf_op jit(solution)/shard_map/ppermute | solution.py:10
  216.5 12.2 %collective-permute-done.10 = f32[256,512]{1,0:T(8,128)S(1)} collective-permute-done((f32[256,512]{1,0:T(8,128)S(1)}, f32[256,512]{1,0:T(8,128)S(1)}, u32[]{:S(2)}, u32[]{:S(2)}) %collective-permute-start.10) | collective-permute-done | bytes 524320 | tf_op jit(solution)/shard_map/ppermute | solution.py:10
  228.8 12.2 %collective-permute-done.11 = f32[256,512]{1,0:T(8,128)S(1)} collective-permute-done((f32[256,512]{1,0:T(8,128)S(1)}, f32[256,512]{1,0:T(8,128)S(1)}, u32[]{:S(2)}, u32[]{:S(2)}) %collective-permute-start.11) | collective-permute-done | bytes 524320 | tf_op jit(solution)/shard_map/ppermute | solution.py:10
  243.5 9.7 %collective-permute-done.12 = f32[256,512]{1,0:T(8,128)S(1)} collective-permute-done((f32[256,512]{1,0:T(8,128)S(1)}, f32[256,512]{1,0:T(8,128)S(1)}, u32[]{:S(2)}, u32[]{:S(2)}) %collective-permute-start.12) | collective-permute-done | bytes 524320 | tf_op jit(solution)/shard_map/ppermute | solution.py:10
  255.7 9.7 %collective-permute-done.13 = f32[256,512]{1,0:T(8,128)S(1)} collective-permute-done((f32[256,512]{1,0:T(8,128)S(1)}, f32[256,512]{1,0:T(8,128)S(1)}, u32[]{:S(2)}, u32[]{:S(2)}) %collective-permute-start.13) | collective-permute-done | bytes 524320 | tf_op jit(solution)/shard_map/ppermute | solution.py:10
  266.3 4.5 %bitcast_multiply_fusion.1 = f32[2048,512]{1,0:T(8,128)} fusion(f32[8,256,512]{2,1,0:T(8,128)} %bitcast_dynamic-update-slice_fusion, f32[2048]{0:T(1024)S(1)} %broadcast_select_fusion), kind=kLoop, calls=%fused_computation.25 | loop fusion | flops 1048576 | bytes 8396800 | tf_op jit(solution)/shard_map/mul | solution.py:61
  270.7 13.9 %scatter_custom_fusion = f32[512,512]{1,0:T(8,128)S(1)} fusion(s32[2048]{0:T(1024)S(1)} %bitcast.183, f32[2048,512]{1,0:T(8,128)} %bitcast_multiply_fusion.1, f32[]{:T(128)} %constant.51.clone.1), kind=kCustom, calls=%fused_computation.62 | custom fusion | flops 1048576 | bytes 1049088 | tf_op jit(solution)/shard_map/scatter-add | solution.py:65
  285.0 31.4 %fusion.1 = bf16[64,512,128]{2,1,0:T(8,128)(2,1)S(1)} fusion(f32[64,512,128]{2,1,0:T(8,128)} %fusion.2, f32[512,512]{0,1:T(8,128)S(1)} %copy.41, f32[128,8]{0,1:T(8,128)S(1)} %copy-done.9), kind=kOutput, calls=%fused_computation.5 | convolution fusion | flops 440401920 | bytes 26218496 | tf_op jit(solution)/shard_map/cln,jn->lcj/dot_general | solution.py:67
  316.4 7.4 %fusion.48 = f32[64,512,128]{2,1,0:T(8,128)} fusion(bf16[64,512,128]{2,1,0:T(8,128)(2,1)S(1)} %fusion.1, bf16[3,128,128]{2,1,0:T(8,128)(2,1)S(1)} %multiply_convert_fusion), kind=kOutput, calls=%fused_computation.73 | convolution fusion | flops 1056964608 | bytes 25198592 | tf_op jit(solution)/shard_map/lcj,ij->lci/dot_general | solution.py:76
  323.9 8.3 %fusion.49 = f32[64,512,128]{2,1,0:T(8,128)} fusion(bf16[64,512,128]{2,1,0:T(8,128)(2,1)S(1)} %fusion.1, bf16[3,128,128]{2,1,0:T(8,128)(2,1)S(1)} %multiply_convert_fusion), kind=kOutput, calls=%fused_computation.74 | convolution fusion | flops 1073741824 | bytes 25198592 | tf_op jit(solution)/shard_map/lcj,ij->lci/dot_general | solution.py:76
  332.2 2.4 fusion.23
  334.6 2.4 fusion.26
  337.0 2.4 fusion.29
  340.6 74.6 %psum.7 = f32[3,8,16,16]{3,2,1,0:T(8,128)} all-reduce(f32[3,8,16,16]{3,2,1,0:T(8,128)S(1)} %bitcast.179), channel_id=1, replica_groups=mesh['lon'=16,'lat'=8] {'lon','lat'}, use_global_device_ids=true, to_apply=%region_1.2 | all-reduce | flops 6144 | bytes 49152 | tf_op jit(solution)/shard_map/psum | solution.py:90
  415.3 17.8 %fusion.17 = bf16[1,1,64,512,128]{4,3,2,1,0:T(8,128)(2,1)} fusion(bf16[64,512,128]{2,1,0:T(8,128)(2,1)} %copy-done.2, f32[64,512,128]{2,1,0:T(8,128)} %fusion.48, f32[64,512,128]{2,1,0:T(8,128)} %fusion.49, bf16[3,128,128]{2,1,0:T(8,128)(2,1)S(1)} %multiply_convert_fusion), kind=kOutput, calls=%fused_computation.24 | convolution fusion | flops 1069547520 | bytes 50364416 | tf_op jit(solution)/shard_map/lcj,ij->lci/dot_general | solution.py:76
  (82 shorter events, 19.9 us)
Async XLA Ops:
  0.6 177.1 %copy-start = (f32[256,64,8]{0,2,1:T(8,128)S(1)}, f32[256,64,8]{0,2,1:T(8,128)}, u32[]{:S(2)}) copy-start(f32[256,64,8]{0,2,1:T(8,128)} %param.12) | copy-start | bytes 1572868
  14.0 11.5 %copy-start.6 = (s32[1,1,8,256]{3,2,1,0:T(8,128)S(1)}, s32[1,1,8,256]{3,2,1,0:T(8,128)}, u32[]{:S(2)}) copy-start(s32[1,1,8,256]{3,2,1,0:T(8,128)} %param.13) | copy-start | bytes 24580
  25.5 21.0 %copy-start.9 = (f32[128,8]{0,1:T(8,128)S(1)}, f32[128,8]{0,1:T(8,128)}, u32[]{:S(2)}) copy-start(f32[128,8]{0,1:T(8,128)} %param.11) | copy-start | bytes 12292
  46.5 21.5 %copy-start.8 = (s32[1,1,256]{2,1,0:T(1,128)S(1)}, s32[1,1,256]{2,1,0:T(1,128)}, u32[]{:S(2)}) copy-start(s32[1,1,256]{2,1,0:T(1,128)} %param.14) | copy-start | bytes 3076
  94.7 9.5 %copy-start.7 = (f32[1,1,8,256]{3,2,1,0:T(8,128)S(1)}, f32[1,1,8,256]{3,2,1,0:T(8,128)}, u32[]{:S(2)}) copy-start(f32[1,1,8,256]{3,2,1,0:T(8,128)} %param.15) | copy-start | bytes 24580
  104.3 74.1 %copy-start.4 = (f32[1,1,256,256]{3,2,1,0:T(8,128)S(1)}, f32[1,1,256,256]{3,2,1,0:T(8,128)}, u32[]{:S(2)}) copy-start(f32[1,1,256,256]{3,2,1,0:T(8,128)} %param.16) | copy-start | bytes 786436
  104.3 74.1 %copy-start.5 = (f32[1,1,256,256]{3,2,1,0:T(8,128)S(1)}, f32[1,1,256,256]{3,2,1,0:T(8,128)}, u32[]{:S(2)}) copy-start(f32[1,1,256,256]{3,2,1,0:T(8,128)} %param.17) | copy-start | bytes 786436
  107.0 8.7 %collective-permute-start = (f32[256,512]{1,0:T(8,128)S(1)}, f32[256,512]{1,0:T(8,128)S(1)}, u32[]{:S(2)}, u32[]{:S(2)}) collective-permute-start(f32[256,512]{1,0:T(8,128)S(1)} %slice_bitcast_fusion.7), channel_id=1, source_target_pairs={{0,120},{8,0},{16,8},{24,16},{32,24},{40,32},{48,40},{56,48},{64,5... | collective-permute-start | bytes 1572872 | tf_op jit(solution)/shard_map/ppermute | solution.py:10
  115.8 8.7 %collective-permute-start.1 = (f32[256,512]{1,0:T(8,128)S(1)}, f32[256,512]{1,0:T(8,128)S(1)}, u32[]{:S(2)}, u32[]{:S(2)}) collective-permute-start(f32[256,512]{1,0:T(8,128)S(1)} %fusion.41), channel_id=1, source_target_pairs={{0,120},{8,0},{16,8},{24,16},{32,24},{40,32},{48,40},{56,48},{64,5... | collective-permute-start | bytes 1572872 | tf_op jit(solution)/shard_map/ppermute | solution.py:10
  124.5 8.7 %collective-permute-start.2 = (f32[256,512]{1,0:T(8,128)S(1)}, f32[256,512]{1,0:T(8,128)S(1)}, u32[]{:S(2)}, u32[]{:S(2)}) collective-permute-start(f32[256,512]{1,0:T(8,128)S(1)} %fusion.40), channel_id=1, source_target_pairs={{0,120},{8,0},{16,8},{24,16},{32,24},{40,32},{48,40},{56,48},{64,5... | collective-permute-start | bytes 1572872 | tf_op jit(solution)/shard_map/ppermute | solution.py:10
  133.3 8.7 %collective-permute-start.3 = (f32[256,512]{1,0:T(8,128)S(1)}, f32[256,512]{1,0:T(8,128)S(1)}, u32[]{:S(2)}, u32[]{:S(2)}) collective-permute-start(f32[256,512]{1,0:T(8,128)S(1)} %fusion.39), channel_id=1, source_target_pairs={{0,120},{8,0},{16,8},{24,16},{32,24},{40,32},{48,40},{56,48},{64,5... | collective-permute-start | bytes 1572872 | tf_op jit(solution)/shard_map/ppermute | solution.py:10
  142.0 10.7 %collective-permute-start.4 = (f32[256,512]{1,0:T(8,128)S(1)}, f32[256,512]{1,0:T(8,128)S(1)}, u32[]{:S(2)}, u32[]{:S(2)}) collective-permute-start(f32[256,512]{1,0:T(8,128)S(1)} %fusion.38), channel_id=1, source_target_pairs={{0,120},{8,0},{16,8},{24,16},{32,24},{40,32},{48,40},{56,48},{64,5... | collective-permute-start | bytes 1572872 | tf_op jit(solution)/shard_map/ppermute | solution.py:10
  152.9 12.3 %collective-permute-start.5 = (f32[256,512]{1,0:T(8,128)S(1)}, f32[256,512]{1,0:T(8,128)S(1)}, u32[]{:S(2)}, u32[]{:S(2)}) collective-permute-start(f32[256,512]{1,0:T(8,128)S(1)} %fusion.37), channel_id=1, source_target_pairs={{0,120},{8,0},{16,8},{24,16},{32,24},{40,32},{48,40},{56,48},{64,5... | collective-permute-start | bytes 1572872 | tf_op jit(solution)/shard_map/ppermute | solution.py:10
  165.2 12.5 %collective-permute-start.6 = (f32[256,512]{1,0:T(8,128)S(1)}, f32[256,512]{1,0:T(8,128)S(1)}, u32[]{:S(2)}, u32[]{:S(2)}) collective-permute-start(f32[256,512]{1,0:T(8,128)S(1)} %fusion.36), channel_id=1, source_target_pairs={{0,120},{8,0},{16,8},{24,16},{32,24},{40,32},{48,40},{56,48},{64,5... | collective-permute-start | bytes 1572872 | tf_op jit(solution)/shard_map/ppermute | solution.py:10
  178.4 92.4 %copy-start.3 = (f32[256,256]{1,0:T(8,128)}, f32[256,256]{1,0:T(8,128)S(1)}, u32[]{:S(2)}) copy-start(f32[256,256]{1,0:T(8,128)S(1)} %fusion.34) | copy-start | bytes 786436
  179.9 12.1 %collective-permute-start.7 = (f32[256,512]{1,0:T(8,128)S(1)}, f32[256,512]{1,0:T(8,128)S(1)}, u32[]{:S(2)}, u32[]{:S(2)}) collective-permute-start(f32[256,512]{1,0:T(8,128)S(1)} %get-tuple-element.6), channel_id=1, source_target_pairs={{0,8},{8,16},{16,24},{24,32},{32,40},{40,48},{48,56},{56,64},{64,7... | collective-permute-start | bytes 1572872 | tf_op jit(solution)/shard_map/ppermute | solution.py:10
  191.9 12.4 %collective-permute-start.8 = (f32[256,512]{1,0:T(8,128)S(1)}, f32[256,512]{1,0:T(8,128)S(1)}, u32[]{:S(2)}, u32[]{:S(2)}) collective-permute-start(f32[256,512]{1,0:T(8,128)S(1)} %collective-permute-done.7), channel_id=1, source_target_pairs={{0,8},{8,16},{16,24},{24,32},{32,40},{40,48},{48,56},{56,64},{64,7... | collective-permute-start | bytes 1572872 | tf_op jit(solution)/shard_map/ppermute | solution.py:10
  204.3 12.2 %collective-permute-start.9 = (f32[256,512]{1,0:T(8,128)S(1)}, f32[256,512]{1,0:T(8,128)S(1)}, u32[]{:S(2)}, u32[]{:S(2)}) collective-permute-start(f32[256,512]{1,0:T(8,128)S(1)} %collective-permute-done.8), channel_id=1, source_target_pairs={{0,8},{8,16},{16,24},{24,32},{32,40},{40,48},{48,56},{56,64},{64,7... | collective-permute-start | bytes 1572872 | tf_op jit(solution)/shard_map/ppermute | solution.py:10
  216.5 12.2 %collective-permute-start.10 = (f32[256,512]{1,0:T(8,128)S(1)}, f32[256,512]{1,0:T(8,128)S(1)}, u32[]{:S(2)}, u32[]{:S(2)}) collective-permute-start(f32[256,512]{1,0:T(8,128)S(1)} %collective-permute-done.9), channel_id=1, source_target_pairs={{0,8},{8,16},{16,24},{24,32},{32,40},{40,48},{48,56},{56,64},{64,7... | collective-permute-start | bytes 1572872 | tf_op jit(solution)/shard_map/ppermute | solution.py:10
  228.8 12.2 %collective-permute-start.11 = (f32[256,512]{1,0:T(8,128)S(1)}, f32[256,512]{1,0:T(8,128)S(1)}, u32[]{:S(2)}, u32[]{:S(2)}) collective-permute-start(f32[256,512]{1,0:T(8,128)S(1)} %collective-permute-done.10), channel_id=1, source_target_pairs={{0,8},{8,16},{16,24},{24,32},{32,40},{40,48},{48,56},{56,64},{64,7... | collective-permute-start | bytes 1572872 | tf_op jit(solution)/shard_map/ppermute | solution.py:10
  241.0 12.2 %collective-permute-start.12 = (f32[256,512]{1,0:T(8,128)S(1)}, f32[256,512]{1,0:T(8,128)S(1)}, u32[]{:S(2)}, u32[]{:S(2)}) collective-permute-start(f32[256,512]{1,0:T(8,128)S(1)} %collective-permute-done.11), channel_id=1, source_target_pairs={{0,8},{8,16},{16,24},{24,32},{32,40},{40,48},{48,56},{56,64},{64,7... | collective-permute-start | bytes 1572872 | tf_op jit(solution)/shard_map/ppermute | solution.py:10
  253.2 12.2 %collective-permute-start.13 = (f32[256,512]{1,0:T(8,128)S(1)}, f32[256,512]{1,0:T(8,128)S(1)}, u32[]{:S(2)}, u32[]{:S(2)}) collective-permute-start(f32[256,512]{1,0:T(8,128)S(1)} %collective-permute-done.12), channel_id=1, source_target_pairs={{0,8},{8,16},{16,24},{24,32},{32,40},{40,48},{48,56},{56,64},{64,7... | collective-permute-start | bytes 1572872 | tf_op jit(solution)/shard_map/ppermute | solution.py:10
  316.4 20.5 %copy-start.2 = (bf16[64,512,128]{2,1,0:T(8,128)(2,1)}, bf16[64,512,128]{2,1,0:T(8,128)(2,1)S(1)}, u32[]{:S(2)}) copy-start(bf16[64,512,128]{2,1,0:T(8,128)(2,1)S(1)} %fusion.1) | copy-start | bytes 25165828
  316.4 15.7 %slice-start = ((s8[8388608]{0:T(1024)(128)(4,1)}), s8[4194304]{0:T(1024)(128)(4,1)S(1)}, s32[]{:S(2)}) async-start(s8[8388608]{0:T(1024)(128)(4,1)} %bitcast.175), calls=%async_computation | async-start | bytes 8388608
  323.9 8.3 %slice-start.1 = ((s8[8388608]{0:T(1024)(128)(4,1)}), s8[4194304]{0:T(1024)(128)(4,1)S(1)}, s32[]{:S(2)}) async-start(s8[8388608]{0:T(1024)(128)(4,1)} %bitcast.175), calls=%async_computation.1 | async-start | bytes 8388608
  415.3 17.8 %copy-start.1 = (f32[256,64,8]{0,2,1:T(8,128)S(1)}, f32[256,64,8]{0,2,1:T(8,128)}, u32[]{:S(2)}) copy-start(f32[256,64,8]{0,2,1:T(8,128)} %param.12) | copy-start | bytes 1572868
where the time goes:
time: 440 us; the launch traced here: 433 us
  matrix products  139 us (32%)
  waiting for transfers between devices  112 us (25%)
  blocking collectives  101 us (23%)
  starting transfers between devices  38.8 us (9%)
  other arithmetic  21.7 us (5%)
  local copies, waits for them, and re-layouts  18.8 us (4%)
    ppermute x14, waiting for transfers between devices, from_behind(): return lax.ppermute(value, axis, pairs)  112 us
    psum x1, blocking collectives, on_device(): grad_conv = lax.psum(grouped, ('lon', 'lat'))  74.6 us
    dot_general x3, matrix products, on_device(): jnp.einsum('lci,ij->lcj', padded[tap:tap + levels], wide[tap], preferred_...  43.8 us
    ppermute x14, starting transfers between devices, from_behind(): return lax.ppermute(value, axis, pairs)  38.8 us
    dot_general x3, matrix products, on_device(): jnp.einsum('lcj,ij->lci', dpad[2 - tap:2 - tap + levels], wide[tap], pref...  33.5 us
    dot_general x1, matrix products, on_device(): jnp.einsum('cln,jn->lcj', dprofile.reshape(ncols, levels, -1), readout, p...  31.4 us
    all_gather x1, blocking collectives, on_device(): every = lax.all_gather(seg_count, 'lon', axis=0, tiled=True)[:, 0, :]  26.7 us
    dot_general x1, matrix products, on_device(): jnp.einsum('lcj,jn->cln', feat, readout, precision=lax.Precision.HIGHEST)  21.1 us
  transfers between devices with their start and end apart: 14, of which 14 were waited for; matrix products, arithmetic and copies ran while one was open for 1% of the time, Pallas kernels for 0%

commit v1 on v0

--- a/solution.py
+++ b/solution.py
@@ -87,7 +87,7 @@
     grad_w = jnp.stack(grads).reshape(taps, groups, width, groups, width)
     eye = jnp.eye(groups, dtype=jnp.float32)
     grouped = jnp.einsum("tgahb,gh->tgab", grad_w, eye)
-    grad_conv = lax.psum(grouped, ("lon", "lat"))
+    grad_conv = jnp.sum(lax.all_gather(grouped, ("lon", "lat")), axis=0)
     return (grad_x.astype(jnp.bfloat16)[None, None], bending[None, None], grad_conv)
 
 

time: 440 us -> 712 us (1.62)
  waiting for transfers between devices: 112 us -> 417 us
  blocking collectives: 101 us -> 26.7 us
  matrix products: 139 us -> 158 us
  between operations: 1.23 us -> 14.8 us
  other arithmetic: 21.7 us -> 31.5 us
    all_gather x0 -> x1, waiting for transfers between devices: none -> 305 us  [on_device(): grad_conv = jnp.sum(lax.all_gather(grouped, ('lon', 'lat')), axis=0)]
    psum x1 -> x0, blocking collectives: 74.6 us -> none  [on_device(): grad_conv = lax.psum(grouped, ('lon', 'lat'))]
    reduce_sum x0 -> x1, other arithmetic: none -> 10.2 us  [on_device(): grad_conv = jnp.sum(lax.all_gather(grouped, ('lon', 'lat')), axis=0)]
    dot_general x3, matrix products: 7.15 us -> 17.3 us  [on_device(): jnp.einsum('lci,lcj->ij', padded[tap:tap + levels], dact, preferred_eleme...]
    dot_general x3, matrix products: 33.5 us -> 41 us  [on_device(): jnp.einsum('lcj,ij->lci', dpad[2 - tap:2 - tap + levels], wide[tap], pref...]
  transfers between devices with their start and end apart: 14 -> 15, of which waited for: 14 -> 15; matrix products, arithmetic and copies ran while one was open for 1% -> 7% of each run, Pallas kernels for 0% -> 0%
where the time goes in v1:
time: 712 us; the launch traced here: 706 us
  waiting for transfers between devices  417 us (59%)
  matrix products  158 us (22%)
  starting transfers between devices  38.8 us (5%)
  other arithmetic  31.5 us (4%)
  blocking collectives  26.7 us (4%)
  local copies, waits for them, and re-layouts  19.5 us (3%)
  between operations  14.8 us (2%)
    all_gather x1, waiting for transfers between devices, on_device(): grad_conv = jnp.sum(lax.all_gather(grouped, ('lon', 'lat')), axis=0)  305 us
    ppermute x14, waiting for transfers between devices, from_behind(): return lax.ppermute(value, axis, pairs)  112 us
    dot_general x3, matrix products, on_device(): jnp.einsum('lci,ij->lcj', padded[tap:tap + levels], wide[tap], preferred_...  43.8 us
    dot_general x3, matrix products, on_device(): jnp.einsum('lcj,ij->lci', dpad[2 - tap:2 - tap + levels], wide[tap], pref...  41 us
    ppermute x14, starting transfers between devices, from_behind(): return lax.ppermute(value, axis, pairs)  38.8 us
    dot_general x1, matrix products, on_device(): jnp.einsum('cln,jn->lcj', dprofile.reshape(ncols, levels, -1), readout, p...  31.7 us
    all_gather x1, blocking collectives, on_device(): every = lax.all_gather(seg_count, 'lon', axis=0, tiled=True)[:, 0, :]  26.7 us
    dot_general x1, matrix products, on_device(): jnp.einsum('lcj,jn->cln', feat, readout, precision=lax.Precision.HIGHEST)  21.4 us
  transfers between devices with their start and end apart: 15, of which 15 were waited for; matrix products, arithmetic and copies ran while one was open for 7% of the time, Pallas kernels for 0%

profile of v1, /device:TPU:1, one launch (start us, length us, event | category | flops | bytes accessed | tf_op | source)
XLA Modules:
  0.0 706.1 jit_solution(10489029747112215659)
XLA Ops:
  9.1 11.4 %fusion.8 = f32[64,512,128]{2,1,0:T(8,128)} fusion(bf16[1,1,64,512,128]{4,3,2,1,0:T(8,128)(2,1)} %param.9, bf16[3,128,128]{2,1,0:T(8,128)(2,1)S(1)} %multiply_convert_fusion), kind=kOutput, calls=%fused_computation.15 | convolution fusion | flops 1056964608 | bytes 25198592 | tf_op jit(solution)/shard_map/lci,ij->lcj/dot_general | solution.py:31
  20.5 11.4 %fusion.12 = f32[128,64,512]{0,2,1:T(8,128)} fusion(bf16[1,1,64,512,128]{4,3,2,1,0:T(8,128)(2,1)} %param.9, bf16[3,128,128]{2,1,0:T(8,128)(2,1)S(1)} %multiply_convert_fusion), kind=kOutput, calls=%fused_computation.19 | convolution fusion | flops 1073741824 | bytes 25198592 | tf_op jit(solution)/shard_map/lci,ij->lcj/dot_general | solution.py:31
  32.1 21.0 %fusion.2 = f32[64,512,128]{2,1,0:T(8,128)} fusion(f32[64,512,128]{2,1,0:T(8,128)} %fusion.8, f32[128,64,512]{0,2,1:T(8,128)} %fusion.12, bf16[1,1,64,512,128]{4,3,2,1,0:T(8,128)(2,1)} %param.9, bf16[3,128,128]{2,1,0:T(8,128)(2,1)S(1)} %multiply_convert_fusion), kind=kOutput, calls=%fused_computation.7 | convolution fusion | flops 1065353216 | bytes 58753024 | tf_op jit(solution)/shard_map/lci,ij->lcj/dot_general | solution.py:31
  53.0 21.4 %fusion.20 = f32[512,512]{0,1:T(8,128)S(1)} fusion(f32[64,512,128]{2,1,0:T(8,128)} %fusion.2, f32[128,8]{0,1:T(8,128)S(1)} %copy-done.9), kind=kOutput, calls=%fused_computation.30 | convolution fusion | flops 419430400 | bytes 17829888 | tf_op jit(solution)/shard_map/lcj,jn->cln/dot_general | solution.py:35
  74.8 26.7 %all_gather.9 = s32[16,1,256]{2,1,0:T(1,128)S(1)} all-gather(s32[1,1,256]{2,1,0:T(1,128)S(1)} %copy-done.8), channel_id=1, replica_groups=mesh['lon'=16,'lat'=8] {'lon'}, dimensions={0}, use_global_device_ids=true | all-gather | bytes 17408 | tf_op jit(solution)/shard_map/all_gather | solution.py:42
  101.6 8.9 %gather_fusion = f32[2048,512]{1,0:T(8,128)} fusion(f32[512,512]{1,0:T(8,128)S(1)} %copy.67, s32[2048]{0:T(1024)S(1)} %broadcast_clamp_fusion), kind=kCustom, calls=%fused_computation | custom fusion | bytes 8396800 | tf_op jit(solution)/shard_map/jit(_take)/gather | solution.py:48
  111.1 2.7 select_multiply_fusion
  114.1 8.4 %collective-permute-done = f32[256,512]{1,0:T(8,128)S(1)} collective-permute-done((f32[256,512]{1,0:T(8,128)S(1)}, f32[256,512]{1,0:T(8,128)S(1)}, u32[]{:S(2)}, u32[]{:S(2)}) %collective-permute-start) | collective-permute-done | bytes 524320 | tf_op jit(solution)/shard_map/ppermute | solution.py:10
  122.7 8.6 %collective-permute-done.1 = f32[256,512]{1,0:T(8,128)S(1)} collective-permute-done((f32[256,512]{1,0:T(8,128)S(1)}, f32[256,512]{1,0:T(8,128)S(1)}, u32[]{:S(2)}, u32[]{:S(2)}) %collective-permute-start.1) | collective-permute-done | bytes 524320 | tf_op jit(solution)/shard_map/ppermute | solution.py:10
  133.3 6.7 collective-permute-done.2
  140.1 5.6 collective-permute-start.3
  145.7 3.1 collective-permute-done.3
  148.9 9.2 %collective-permute-start.4 = (f32[256,512]{1,0:T(8,128)S(1)}, f32[256,512]{1,0:T(8,128)S(1)}, u32[]{:S(2)}, u32[]{:S(2)}) collective-permute-start(f32[256,512]{1,0:T(8,128)S(1)} %fusion.38), channel_id=1, source_target_pairs={{0,120},{8,0},{16,8},{24,16},{32,24},{40,32},{48,40},{56,48},{64,5... | collective-permute-start | bytes 1572872 | tf_op jit(solution)/shard_map/ppermute | solution.py:10
  159.7 10.8 %collective-permute-start.5 = (f32[256,512]{1,0:T(8,128)S(1)}, f32[256,512]{1,0:T(8,128)S(1)}, u32[]{:S(2)}, u32[]{:S(2)}) collective-permute-start(f32[256,512]{1,0:T(8,128)S(1)} %fusion.37), channel_id=1, source_target_pairs={{0,120},{8,0},{16,8},{24,16},{32,24},{40,32},{48,40},{56,48},{64,5... | collective-permute-start | bytes 1572872 | tf_op jit(solution)/shard_map/ppermute | solution.py:10
  172.1 10.9 %collective-permute-start.6 = (f32[256,512]{1,0:T(8,128)S(1)}, f32[256,512]{1,0:T(8,128)S(1)}, u32[]{:S(2)}, u32[]{:S(2)}) collective-permute-start(f32[256,512]{1,0:T(8,128)S(1)} %fusion.36), channel_id=1, source_target_pairs={{0,120},{8,0},{16,8},{24,16},{32,24},{40,32},{48,40},{56,48},{64,5... | collective-permute-start | bytes 1572872 | tf_op jit(solution)/shard_map/ppermute | solution.py:10
  186.6 12.1 %collective-permute-done.7 = f32[256,512]{1,0:T(8,128)S(1)} collective-permute-done((f32[256,512]{1,0:T(8,128)S(1)}, f32[256,512]{1,0:T(8,128)S(1)}, u32[]{:S(2)}, u32[]{:S(2)}) %collective-permute-start.7) | collective-permute-done | bytes 524320 | tf_op jit(solution)/shard_map/ppermute | solution.py:10
  198.7 12.4 %collective-permute-done.8 = f32[256,512]{1,0:T(8,128)S(1)} collective-permute-done((f32[256,512]{1,0:T(8,128)S(1)}, f32[256,512]{1,0:T(8,128)S(1)}, u32[]{:S(2)}, u32[]{:S(2)}) %collective-permute-start.8) | collective-permute-done | bytes 524320 | tf_op jit(solution)/shard_map/ppermute | solution.py:10
  211.1 12.2 %collective-permute-done.9 = f32[256,512]{1,0:T(8,128)S(1)} collective-permute-done((f32[256,512]{1,0:T(8,128)S(1)}, f32[256,512]{1,0:T(8,128)S(1)}, u32[]{:S(2)}, u32[]{:S(2)}) %collective-permute-start.9) | collective-permute-done | bytes 524320 | tf_op jit(solution)/shard_map/ppermute | solution.py:10
  223.3 12.2 %collective-permute-done.10 = f32[256,512]{1,0:T(8,128)S(1)} collective-permute-done((f32[256,512]{1,0:T(8,128)S(1)}, f32[256,512]{1,0:T(8,128)S(1)}, u32[]{:S(2)}, u32[]{:S(2)}) %collective-permute-start.10) | collective-permute-done | bytes 524320 | tf_op jit(solution)/shard_map/ppermute | solution.py:10
  235.6 12.2 %collective-permute-done.11 = f32[256,512]{1,0:T(8,128)S(1)} collective-permute-done((f32[256,512]{1,0:T(8,128)S(1)}, f32[256,512]{1,0:T(8,128)S(1)}, u32[]{:S(2)}, u32[]{:S(2)}) %collective-permute-start.11) | collective-permute-done | bytes 524320 | tf_op jit(solution)/shard_map/ppermute | solution.py:10
  250.3 9.7 %collective-permute-done.12 = f32[256,512]{1,0:T(8,128)S(1)} collective-permute-done((f32[256,512]{1,0:T(8,128)S(1)}, f32[256,512]{1,0:T(8,128)S(1)}, u32[]{:S(2)}, u32[]{:S(2)}) %collective-permute-start.12) | collective-permute-done | bytes 524320 | tf_op jit(solution)/shard_map/ppermute | solution.py:10
  262.5 9.7 %collective-permute-done.13 = f32[256,512]{1,0:T(8,128)S(1)} collective-permute-done((f32[256,512]{1,0:T(8,128)S(1)}, f32[256,512]{1,0:T(8,128)S(1)}, u32[]{:S(2)}, u32[]{:S(2)}) %collective-permute-start.13) | collective-permute-done | bytes 524320 | tf_op jit(solution)/shard_map/ppermute | solution.py:10
  273.0 4.5 bitcast_multiply_fusion.1
  277.5 13.5 %scatter_custom_fusion = f32[512,512]{1,0:T(8,128)S(1)} fusion(s32[2048]{0:T(1024)S(1)} %bitcast.185, f32[2048,512]{1,0:T(8,128)} %bitcast_multiply_fusion.1, f32[]{:T(128)} %constant.52.clone.1), kind=kCustom, calls=%fused_computation.62 | custom fusion | flops 1048576 | bytes 1049088 | tf_op jit(solution)/shard_map/scatter-add | solution.py:65
  291.4 31.7 %fusion.1 = bf16[64,512,128]{2,1,0:T(8,128)(2,1)S(1)} fusion(f32[64,512,128]{2,1,0:T(8,128)} %fusion.2, f32[512,512]{0,1:T(8,128)S(1)} %copy.68, f32[128,8]{0,1:T(8,128)S(1)} %copy-done.9), kind=kOutput, calls=%fused_computation.5 | convolution fusion | flops 440401920 | bytes 26218496 | tf_op jit(solution)/shard_map/cln,jn->lcj/dot_general | solution.py:67
  323.0 8.9 %fusion.23 = bf16[128,128]{1,0:T(8,128)(2,1)S(1)} fusion(bf16[64,512,128]{2,1,0:T(8,128)(2,1)S(1)} %fusion.1, bf16[1,1,64,512,128]{4,3,2,1,0:T(8,128)(2,1)} %param.9), kind=kOutput, calls=%fused_computation.31 | convolution fusion | flops 1056964608 | bytes 16809984 | tf_op jit(solution)/shard_map/lci,lcj->ij/dot_general | solution.py:83
  332.0 6.0 fusion.26
  342.4 11.4 %fusion.48 = f32[64,512,128]{2,1,0:T(8,128)} fusion(bf16[64,512,128]{2,1,0:T(8,128)(2,1)} %copy-done.2, bf16[3,128,128]{2,1,0:T(8,128)(2,1)S(1)} %multiply_convert_fusion), kind=kOutput, calls=%fused_computation.73 | convolution fusion | flops 1056964608 | bytes 25198592 | tf_op jit(solution)/shard_map/lcj,ij->lci/dot_general | solution.py:76
  353.8 11.5 %fusion.49 = f32[64,512,128]{2,1,0:T(8,128)} fusion(bf16[64,512,128]{2,1,0:T(8,128)(2,1)} %copy-done.2, bf16[3,128,128]{2,1,0:T(8,128)(2,1)S(1)} %multiply_convert_fusion), kind=kOutput, calls=%fused_computation.74 | convolution fusion | flops 1073741824 | bytes 25198592 | tf_op jit(solution)/shard_map/lcj,ij->lci/dot_general | solution.py:76
  365.3 18.0 %fusion.17 = bf16[1,1,64,512,128]{4,3,2,1,0:T(8,128)(2,1)} fusion(bf16[64,512,128]{2,1,0:T(8,128)(2,1)} %copy-done.2, f32[64,512,128]{2,1,0:T(8,128)} %fusion.48, f32[64,512,128]{2,1,0:T(8,128)} %fusion.49, bf16[3,128,128]{2,1,0:T(8,128)(2,1)S(1)} %multiply_convert_fusion), kind=kOutput, calls=%fused_computation.24 | convolution fusion | flops 1069547520 | bytes 50364416 | tf_op jit(solution)/shard_map/lcj,ij->lci/dot_general | solution.py:76
  383.3 305.3 %all-gather.3.cloned.1.call-done = f32[384,8,16,16]{3,2,1,0:T(8,128)} async-done(((f32[3,8,16,16]{3,2,1,0:T(8,128)}), f32[384,8,16,16]{3,2,1,0:T(8,128)}) %all-gather.3.cloned.1.call-update) | async-done | bytes 3145744 | tf_op jit(solution)/shard_map/all_gather | solution.py:90
  688.7 10.2 %reduce_sum.9 = f32[3,8,16,16]{3,2,1,0:T(8,128)} reduce(f32[128,3,8,16,16]{4,3,2,1,0:T(8,128)} %bitcast.178, f32[]{:T(128)} %constant.52.clone.1), dimensions={0}, to_apply=%region_1.2 | reduce | flops 780288 | bytes 3170308 | tf_op jit(solution)/shard_map/reduce_sum | solution.py:90
  (85 shorter events, 23.0 us)
Async XLA Ops:
  7.2 177.4 %copy-start = (f32[256,64,8]{0,2,1:T(8,128)S(1)}, f32[256,64,8]{0,2,1:T(8,128)}, u32[]{:S(2)}) copy-start(f32[256,64,8]{0,2,1:T(8,128)} %param.12) | copy-start | bytes 1572868
  7.2 681.5 %all-gather.3.cloned.1.call-start = ((), (), s32[]{:S(2)}) async-start(), calls=%async_computation | async-start | bytes 25362432 | tf_op jit(solution)/shard_map/all_gather | solution.py:90
  20.5 11.5 %copy-start.6 = (s32[1,1,8,256]{3,2,1,0:T(8,128)S(1)}, s32[1,1,8,256]{3,2,1,0:T(8,128)}, u32[]{:S(2)}) copy-start(s32[1,1,8,256]{3,2,1,0:T(8,128)} %param.13) | copy-start | bytes 24580
  32.1 21.0 %copy-start.9 = (f32[128,8]{0,1:T(8,128)S(1)}, f32[128,8]{0,1:T(8,128)}, u32[]{:S(2)}) copy-start(f32[128,8]{0,1:T(8,128)} %param.11) | copy-start | bytes 12292
  53.0 21.8 %copy-start.8 = (s32[1,1,256]{2,1,0:T(1,128)S(1)}, s32[1,1,256]{2,1,0:T(1,128)}, u32[]{:S(2)}) copy-start(s32[1,1,256]{2,1,0:T(1,128)} %param.14) | copy-start | bytes 3076
  101.6 9.5 %copy-start.7 = (f32[1,1,8,256]{3,2,1,0:T(8,128)S(1)}, f32[1,1,8,256]{3,2,1,0:T(8,128)}, u32[]{:S(2)}) copy-start(f32[1,1,8,256]{3,2,1,0:T(8,128)} %param.15) | copy-start | bytes 24580
  111.1 74.0 %copy-start.4 = (f32[1,1,256,256]{3,2,1,0:T(8,128)S(1)}, f32[1,1,256,256]{3,2,1,0:T(8,128)}, u32[]{:S(2)}) copy-start(f32[1,1,256,256]{3,2,1,0:T(8,128)} %param.16) | copy-start | bytes 786436
  111.1 74.0 %copy-start.5 = (f32[1,1,256,256]{3,2,1,0:T(8,128)S(1)}, f32[1,1,256,256]{3,2,1,0:T(8,128)}, u32[]{:S(2)}) copy-start(f32[1,1,256,256]{3,2,1,0:T(8,128)} %param.17) | copy-start | bytes 786436
  113.8 8.7 %collective-permute-start = (f32[256,512]{1,0:T(8,128)S(1)}, f32[256,512]{1,0:T(8,128)S(1)}, u32[]{:S(2)}, u32[]{:S(2)}) collective-permute-start(f32[256,512]{1,0:T(8,128)S(1)} %slice_bitcast_fusion.7), channel_id=1, source_target_pairs={{0,120},{8,0},{16,8},{24,16},{32,24},{40,32},{48,40},{56,48},{64,5... | collective-permute-start | bytes 1572872 | tf_op jit(solution)/shard_map/ppermute | solution.py:10
  122.6 8.7 %collective-permute-start.1 = (f32[256,512]{1,0:T(8,128)S(1)}, f32[256,512]{1,0:T(8,128)S(1)}, u32[]{:S(2)}, u32[]{:S(2)}) collective-permute-start(f32[256,512]{1,0:T(8,128)S(1)} %fusion.41), channel_id=1, source_target_pairs={{0,120},{8,0},{16,8},{24,16},{32,24},{40,32},{48,40},{56,48},{64,5... | collective-permute-start | bytes 1572872 | tf_op jit(solution)/shard_map/ppermute | solution.py:10
  131.3 8.7 %collective-permute-start.2 = (f32[256,512]{1,0:T(8,128)S(1)}, f32[256,512]{1,0:T(8,128)S(1)}, u32[]{:S(2)}, u32[]{:S(2)}) collective-permute-start(f32[256,512]{1,0:T(8,128)S(1)} %fusion.40), channel_id=1, source_target_pairs={{0,120},{8,0},{16,8},{24,16},{32,24},{40,32},{48,40},{56,48},{64,5... | collective-permute-start | bytes 1572872 | tf_op jit(solution)/shard_map/ppermute | solution.py:10
  140.1 8.7 %collective-permute-start.3 = (f32[256,512]{1,0:T(8,128)S(1)}, f32[256,512]{1,0:T(8,128)S(1)}, u32[]{:S(2)}, u32[]{:S(2)}) collective-permute-start(f32[256,512]{1,0:T(8,128)S(1)} %fusion.39), channel_id=1, source_target_pairs={{0,120},{8,0},{16,8},{24,16},{32,24},{40,32},{48,40},{56,48},{64,5... | collective-permute-start | bytes 1572872 | tf_op jit(solution)/shard_map/ppermute | solution.py:10
  148.9 10.7 %collective-permute-start.4 = (f32[256,512]{1,0:T(8,128)S(1)}, f32[256,512]{1,0:T(8,128)S(1)}, u32[]{:S(2)}, u32[]{:S(2)}) collective-permute-start(f32[256,512]{1,0:T(8,128)S(1)} %fusion.38), channel_id=1, source_target_pairs={{0,120},{8,0},{16,8},{24,16},{32,24},{40,32},{48,40},{56,48},{64,5... | collective-permute-start | bytes 1572872 | tf_op jit(solution)/shard_map/ppermute | solution.py:10
  159.7 12.3 %collective-permute-start.5 = (f32[256,512]{1,0:T(8,128)S(1)}, f32[256,512]{1,0:T(8,128)S(1)}, u32[]{:S(2)}, u32[]{:S(2)}) collective-permute-start(f32[256,512]{1,0:T(8,128)S(1)} %fusion.37), channel_id=1, source_target_pairs={{0,120},{8,0},{16,8},{24,16},{32,24},{40,32},{48,40},{56,48},{64,5... | collective-permute-start | bytes 1572872 | tf_op jit(solution)/shard_map/ppermute | solution.py:10
  172.1 12.5 %collective-permute-start.6 = (f32[256,512]{1,0:T(8,128)S(1)}, f32[256,512]{1,0:T(8,128)S(1)}, u32[]{:S(2)}, u32[]{:S(2)}) collective-permute-start(f32[256,512]{1,0:T(8,128)S(1)} %fusion.36), channel_id=1, source_target_pairs={{0,120},{8,0},{16,8},{24,16},{32,24},{40,32},{48,40},{56,48},{64,5... | collective-permute-start | bytes 1572872 | tf_op jit(solution)/shard_map/ppermute | solution.py:10
  185.2 92.4 %copy-start.3 = (f32[256,256]{1,0:T(8,128)}, f32[256,256]{1,0:T(8,128)S(1)}, u32[]{:S(2)}) copy-start(f32[256,256]{1,0:T(8,128)S(1)} %fusion.34) | copy-start | bytes 786436
  186.6 12.1 %collective-permute-start.7 = (f32[256,512]{1,0:T(8,128)S(1)}, f32[256,512]{1,0:T(8,128)S(1)}, u32[]{:S(2)}, u32[]{:S(2)}) collective-permute-start(f32[256,512]{1,0:T(8,128)S(1)} %get-tuple-element.6), channel_id=1, source_target_pairs={{0,8},{8,16},{16,24},{24,32},{32,40},{40,48},{48,56},{56,64},{64,7... | collective-permute-start | bytes 1572872 | tf_op jit(solution)/shard_map/ppermute | solution.py:10
  198.7 12.4 %collective-permute-start.8 = (f32[256,512]{1,0:T(8,128)S(1)}, f32[256,512]{1,0:T(8,128)S(1)}, u32[]{:S(2)}, u32[]{:S(2)}) collective-permute-start(f32[256,512]{1,0:T(8,128)S(1)} %collective-permute-done.7), channel_id=1, source_target_pairs={{0,8},{8,16},{16,24},{24,32},{32,40},{40,48},{48,56},{56,64},{64,7... | collective-permute-start | bytes 1572872 | tf_op jit(solution)/shard_map/ppermute | solution.py:10
  211.1 12.2 %collective-permute-start.9 = (f32[256,512]{1,0:T(8,128)S(1)}, f32[256,512]{1,0:T(8,128)S(1)}, u32[]{:S(2)}, u32[]{:S(2)}) collective-permute-start(f32[256,512]{1,0:T(8,128)S(1)} %collective-permute-done.8), channel_id=1, source_target_pairs={{0,8},{8,16},{16,24},{24,32},{32,40},{40,48},{48,56},{56,64},{64,7... | collective-permute-start | bytes 1572872 | tf_op jit(solution)/shard_map/ppermute | solution.py:10
  223.3 12.2 %collective-permute-start.10 = (f32[256,512]{1,0:T(8,128)S(1)}, f32[256,512]{1,0:T(8,128)S(1)}, u32[]{:S(2)}, u32[]{:S(2)}) collective-permute-start(f32[256,512]{1,0:T(8,128)S(1)} %collective-permute-done.9), channel_id=1, source_target_pairs={{0,8},{8,16},{16,24},{24,32},{32,40},{40,48},{48,56},{56,64},{64,7... | collective-permute-start | bytes 1572872 | tf_op jit(solution)/shard_map/ppermute | solution.py:10
  235.6 12.2 %collective-permute-start.11 = (f32[256,512]{1,0:T(8,128)S(1)}, f32[256,512]{1,0:T(8,128)S(1)}, u32[]{:S(2)}, u32[]{:S(2)}) collective-permute-start(f32[256,512]{1,0:T(8,128)S(1)} %collective-permute-done.10), channel_id=1, source_target_pairs={{0,8},{8,16},{16,24},{24,32},{32,40},{40,48},{48,56},{56,64},{64,7... | collective-permute-start | bytes 1572872 | tf_op jit(solution)/shard_map/ppermute | solution.py:10
  247.8 12.2 %collective-permute-start.12 = (f32[256,512]{1,0:T(8,128)S(1)}, f32[256,512]{1,0:T(8,128)S(1)}, u32[]{:S(2)}, u32[]{:S(2)}) collective-permute-start(f32[256,512]{1,0:T(8,128)S(1)} %collective-permute-done.11), channel_id=1, source_target_pairs={{0,8},{8,16},{16,24},{24,32},{32,40},{40,48},{48,56},{56,64},{64,7... | collective-permute-start | bytes 1572872 | tf_op jit(solution)/shard_map/ppermute | solution.py:10
  260.0 12.2 %collective-permute-start.13 = (f32[256,512]{1,0:T(8,128)S(1)}, f32[256,512]{1,0:T(8,128)S(1)}, u32[]{:S(2)}, u32[]{:S(2)}) collective-permute-start(f32[256,512]{1,0:T(8,128)S(1)} %collective-permute-done.12), channel_id=1, source_target_pairs={{0,8},{8,16},{16,24},{24,32},{32,40},{40,48},{48,56},{56,64},{64,7... | collective-permute-start | bytes 1572872 | tf_op jit(solution)/shard_map/ppermute | solution.py:10
  323.0 14.9 %copy-start.2 = (bf16[64,512,128]{2,1,0:T(8,128)(2,1)}, bf16[64,512,128]{2,1,0:T(8,128)(2,1)S(1)}, u32[]{:S(2)}) copy-start(bf16[64,512,128]{2,1,0:T(8,128)(2,1)S(1)} %fusion.1) | copy-start | bytes 25165828
  323.0 14.9 %slice-start = ((s8[8388608]{0:T(1024)(128)(4,1)}), s8[4194304]{0:T(1024)(128)(4,1)S(1)}, s32[]{:S(2)}) async-start(s8[8388608]{0:T(1024)(128)(4,1)} %bitcast.176), calls=%async_computation.1 | async-start | bytes 8388608
  331.9 6.0 slice-start.1
  688.6 10.2 %copy-start.1 = (f32[256,64,8]{0,2,1:T(8,128)S(1)}, f32[256,64,8]{0,2,1:T(8,128)}, u32[]{:S(2)}) copy-start(f32[256,64,8]{0,2,1:T(8,128)} %param.12) | copy-start | bytes 1572868
Sparse Core Ops, SparseCore 0:
  342.5 346.1 all-gather.2
